TPU v7x, 32 devices: a whole 2x2x4 slice. The times are simulated.
32 devices in a mesh: groups: 2 (over y), dp: 4 (over z), gy: 4 (over x, core).
Axes of the slice: x: 2, y: 2, z: 4, core: 2. Of those that a mesh axis runs over, the one named last changes fastest.
Arguments:
- fields: bfloat16 [8, 96, 32, 512], P(('groups', 'dp'), None, 'gy'), parts along dimension 0, may hold values from -6 to 6
- kernel_taps: bfloat16 [27, 96, 96], replicated, may hold values from -0.125 to 0.125
- bias_vector: float32 [96], replicated, may hold values from -4 to 4
- cotangent: bfloat16 [8, 96, 32, 512], P(('groups', 'dp'), None, 'gy'), parts along dimension 0, may hold values from -6 to 6
Outputs:
- activated: bfloat16 [8, 96, 32, 512], P(('groups', 'dp'), None, 'gy'), parts along dimension 0
- field_grad: bfloat16 [8, 96, 32, 512], P(('groups', 'dp'), None, 'gy'), parts along dimension 0
- kernel_grad: float32 [54, 96, 96], P('groups'), parts along dimension 0
- bias_grad: float32 [192], P('groups'), parts along dimension 0
There are 2 independent parts, one for each index of `groups`. A program takes and returns all parts, laid end to end along the dimension named above; an argument that names none is the same for every part. Nothing has to cross between parts.
All inputs are finite; a program needn't handle non-finite values.
Results may differ from a plain program's by a relative error of at most 0.0049.
Values may be sent and summed in bfloat16 or wider, within the bound.
A program may use at most 64 MiB of HBM per device.

v0:
```python
import jax
import jax.numpy as jnp
from jax import lax
from jax.sharding import PartitionSpec as P

CZ = 16


clip_norm = 512.0


def padded_2(x, sides, width):
    for axis, dim in sides:
        count, length = (lax.axis_size(axis), x.shape[dim])
        up = [(i, (i + 1) % count) for i in range(count - 1)]
        down = [(j, i) for i, j in up]
        last = lax.slice_in_dim(x, length - width, length, axis=dim)
        initial = lax.slice_in_dim(x, 0, width, axis=dim)
        before = lax.ppermute(last, axis, up)
        after = lax.ppermute(initial, axis, down)
        x = jnp.concatenate([before, x, after], axis=dim)
    return x


def shift_cells(values, step_x, step_z):
    cells = values.shape[-1]
    offset = step_x * CZ + step_z
    blank = jnp.zeros(values.shape[:-1] + (abs(offset),), values.dtype)
    if offset > 0:
        moved_cells = jnp.concatenate([values[..., offset:], blank], axis=-1)
    elif offset < 0:
        moved_cells = jnp.concatenate([blank, values[..., : cells + offset]], axis=-1)
    else:
        moved_cells = values
    depth = jnp.arange(cells) % CZ
    valid_cells = (depth + step_z >= 0) & (depth + step_z < CZ)
    return jnp.where(valid_cells, moved_cells, jnp.zeros((), values.dtype))


def tap_patches(padded, tap_y, tap_x, row_count, direction):
    first_row = 2 * tap_y if direction > 0 else 4 - 2 * tap_y
    window = padded[..., first_row : first_row + row_count, :]
    pieces = [
        shift_cells(window, direction * 2 * (tap_x - 1), direction * 2 * (tap_z - 1))
        for tap_z in range(3)
    ]
    return jnp.concatenate(pieces, axis=-3)


def weight_block(kernel_taps, tap_y, tap_x, direction):
    first_tap = 9 * tap_y + 3 * tap_x
    matrices = [kernel_taps[first_tap + tap_z] for tap_z in range(3)]
    if direction < 0:
        matrices = [one_tap.T for one_tap in matrices]
    return jnp.concatenate(matrices, axis=1)


def convolve(padded, kernel_taps, row_count, direction):
    accum = jnp.zeros(
        (padded.shape[0], kernel_taps.shape[1], row_count, padded.shape[-1]), jnp.float32
    )
    for tap_y in range(3):
        for tap_x in range(3):
            patches = tap_patches(padded, tap_y, tap_x, row_count, direction)
            block = weight_block(kernel_taps, tap_y, tap_x, direction)
            accum = accum + jnp.einsum(
                "ok,rkyp->royp", block, patches, preferred_element_type=jnp.float32
            )
    return accum


def kernel_grads(padded_in, slope, row_count):
    channels = slope.shape[1]
    results = []
    for tap_y in range(3):
        for tap_x in range(3):
            patches = tap_patches(padded_in, tap_y, tap_x, row_count, 1)
            grads = jnp.einsum("royp,rkyp->ok", slope, patches, preferred_element_type=jnp.float32)
            results.append(grads.reshape(channels, 3, channels).transpose(1, 0, 2))
    return jnp.concatenate(results, axis=0)


def gelu_slope(pre_act, upstream):
    unused, pull_back = jax.vjp(jax.nn.gelu, pre_act)
    return pull_back(upstream.astype(jnp.float32))[0].astype(jnp.bfloat16)


def shards(fields, kernel_taps, bias_vector, cotangent):
    row_count = fields.shape[2]
    padded_in = padded_2(fields, (("gy", 2),), 2)
    pre_act = convolve(padded_in, kernel_taps, row_count, 1) + bias_vector[:, None, None]
    activated = jax.nn.gelu(pre_act).astype(jnp.bfloat16)
    slope = gelu_slope(pre_act, cotangent)
    padded_slope = padded_2(slope, (("gy", 2),), 2)
    field_grad = convolve(padded_slope, kernel_taps, row_count, -1).astype(jnp.bfloat16)
    local_kernel = kernel_grads(padded_in, slope, row_count)
    local_bias = jnp.sum(slope.astype(jnp.float32), axis=(0, 2, 3))
    wsum, bsum = lax.psum((local_kernel, local_bias), ("dp", "gy"))
    grad_norm = jnp.sqrt(jnp.sum(wsum * wsum) + jnp.sum(bsum * bsum) + 1e-06)
    factor = jnp.minimum(1.0, clip_norm / grad_norm)
    kernel_grad = wsum * factor
    return (activated, field_grad, kernel_grad, bsum * factor)


def solution(mesh):
    in_specs = (
        P(("groups", "dp"), None, "gy", None),
        P(),
        P(),
        P(("groups", "dp"), None, "gy", None),
    )
    out_specs = (
        P(("groups", "dp"), None, "gy", None),
        P(("groups", "dp"), None, "gy", None),
        P("groups", None, None),
        P("groups"),
    )
    return jax.shard_map(shards, mesh=mesh, in_specs=in_specs, out_specs=out_specs, check_vma=False)
```

profile of v0, /device:TPU:0, one launch (start us, length us, event | category | flops | bytes accessed | tf_op | source)
XLA Modules:
  0.0 187.8 jit_solution(15867438270472809461)
XLA Ops:
  7.2 1.8 fusion.229
  9.1 1.3 collective-permute-start.1
  10.4 3.0 %collective-permute-start = (bf16[1,96,2,512]{3,1,2,0:T(8,128)(2,1)S(1)}, bf16[1,96,2,512]{3,1,2,0:T(8,128)(2,1)S(1)}, u32[]{:S(2)}, u32[]{:S(2)}) collective-permute-start(bf16[1,96,2,512]{3,1,2,0:T(8,128)(2,1)S(1)} %copy.82), channel_id=1, source_target_pairs={{0,1},{1,2},{2,3},{4,5},{5,6},{6,7},{8,9},{9,10},{10,11},{12,13},{... | collective-permute-start | bytes 589832 | tf_op jit(solution)/shard_map/ppermute | solution.py:19
  13.5 1.8 slice_bitcast_fusion.4
  15.3 0.7 slice_bitcast_fusion.2
  19.5 1.0 constant_dynamic-update-slice_fusion
  20.5 0.4 fusion.220
  21.7 0.4 fusion.225
  23.2 0.4 fusion.222
  23.5 3.5 %pad_select_fusion.26 = (bf16[1,96,8,512]{3,1,2,0:T(8,128)(2,1)S(1)}, bf16[1,96,8,512]{3,1,2,0:T(8,128)(2,1)S(1)}, bf16[1,96,8,512]{3,1,2,0:T(8,128)(2,1)S(1)}, ...) fusion(bf16[1,96,8,510]{3,1,2,0:T(8,128)(2,1)S(1)} %get-tuple-e, ...), kind=kLoop, calls=%fused_computation.216 | loop fusion | flops 3538944 | bytes 13852160 | tf_op jit(solution)/shard_map/jit(_where)/select_n | solution.py:37
  27.0 2.4 %pad_select_fusion.25 = (bf16[1,96,8,512]{3,1,2,0:T(8,128)(2,1)S(1)}, bf16[1,96,8,512]{3,1,2,0:T(8,128)(2,1)S(1)}, bf16[1,96,8,512]{3,1,2,0:T(8,128)(2,1)S(1)}, ...) fusion(bf16[1,96,8,510]{3,1,2,0:T(8,128)(2,1)S(1)} %get-tuple-e, ...), kind=kLoop, calls=%fused_computation.215 | loop fusion | flops 3538944 | bytes 13852160 | tf_op jit(solution)/shard_map/jit(_where)/select_n | solution.py:37
  29.5 2.0 %fusion.55 = f32[8,512,96]{1,2,0:T(8,128)} fusion(bf16[96,96]{1,0:T(8,128)(2,1)S(1)} %get-tuple-element.118, bf16[96,96]{1,0:T(8,128)(2,1)S(1)} %get-tuple-element.119, bf16[96,96]{1,0:T(8,128)(2,1)S(1)} %get-tuple-element.120, bf16[1,96,8,512]{3,1,2,0:T(8,128)(2,1)S(1)} %get-tuple-element.173, bf16[1,96,8,512]{3,1,2,0:T(8,128)(2,1)S(1)} %get-tuple-element.131, ...), kind=kOutput, calls=%fused_computation.89 | convolution fusion | flops 233736192 | bytes 3987456 | tf_op jit(solution)/shard_map/ok,rkyp->royp/dot_general | solution.py:66
  31.5 0.5 pad_maximum_fusion.3
  32.0 1.9 %fusion.53 = f32[8,512,96]{1,2,0:T(8,128)} fusion(bf16[96,96]{1,0:T(8,128)(2,1)S(1)} %get-tuple-element.114, bf16[96,96]{1,0:T(8,128)(2,1)S(1)} %get-tuple-element.116, bf16[96,96]{1,0:T(8,128)(2,1)S(1)} %get-tuple-element.117, bf16[1,96,8,512]{3,1,2,0:T(8,128)(2,1)S(1)} %get-tuple-element.174, bf16[1,96,8,512]{3,1,2,0:T(8,128)(2,1)S(1)} %get-tuple-element.65, ...), kind=kOutput, calls=%fused_computation.87 | convolution fusion | flops 233736192 | bytes 3987456 | tf_op jit(solution)/shard_map/ok,rkyp->royp/dot_general | solution.py:66
  33.9 1.6 slice_select_fusion
  35.5 1.9 %fusion.57 = f32[8,512,96]{1,2,0:T(8,128)} fusion(bf16[96,96]{1,0:T(8,128)(2,1)S(1)} %get-tuple-element.121, bf16[96,96]{1,0:T(8,128)(2,1)S(1)} %get-tuple-element.122, bf16[96,96]{1,0:T(8,128)(2,1)S(1)} %get-tuple-element.123, bf16[1,96,8,512]{3,1,2,0:T(8,128)(2,1)S(1)} %get-tuple-element.172, bf16[1,96,8,512]{3,1,2,0:T(8,128)(2,1)S(1)} %get-tuple-element.166, ...), kind=kOutput, calls=%fused_computation.91 | convolution fusion | flops 233736192 | bytes 3987456 | tf_op jit(solution)/shard_map/ok,rkyp->royp/dot_general | solution.py:66
  37.4 0.5 pad_maximum_fusion.2
  37.9 1.9 %fusion.51 = f32[8,512,96]{1,2,0:T(8,128)} fusion(bf16[96,96]{1,0:T(8,128)(2,1)S(1)} %get-tuple-element.111, bf16[96,96]{1,0:T(8,128)(2,1)S(1)} %get-tuple-element.112, bf16[96,96]{1,0:T(8,128)(2,1)S(1)} %get-tuple-element.113, bf16[1,96,8,512]{3,1,2,0:T(8,128)(2,1)S(1)} %get-tuple-element.175, bf16[1,96,8,512]{3,1,2,0:T(8,128)(2,1)S(1)} %get-tuple-element.132, ...), kind=kOutput, calls=%fused_computation.85 | convolution fusion | flops 233736192 | bytes 3987456 | tf_op jit(solution)/shard_map/ok,rkyp->royp/dot_general | solution.py:66
  40.0 1.9 %fusion.45 = f32[8,512,96]{1,2,0:T(8,128)} fusion(bf16[96,96]{1,0:T(8,128)(2,1)S(1)} %get-tuple-element.129, bf16[96,96]{1,0:T(8,128)(2,1)S(1)} %get-tuple-element.130, bf16[96,96]{1,0:T(8,128)(2,1)S(1)} %get-tuple-element.104, bf16[1,96,8,512]{3,1,2,0:T(8,128)(2,1)S(1)} %get-tuple-element.177, bf16[1,96,8,512]{3,1,2,0:T(8,128)(2,1)S(1)} %get-tuple-element.168, ...), kind=kOutput, calls=%fused_computation.79 | convolution fusion | flops 233736192 | bytes 3987456 | tf_op jit(solution)/shard_map/ok,rkyp->royp/dot_general | solution.py:66
  41.9 1.9 %fusion.59 = f32[8,512,96]{1,2,0:T(8,128)} fusion(bf16[96,96]{1,0:T(8,128)(2,1)S(1)} %get-tuple-element.124, bf16[96,96]{1,0:T(8,128)(2,1)S(1)} %get-tuple-element.125, bf16[96,96]{1,0:T(8,128)(2,1)S(1)} %get-tuple-element.115, bf16[1,96,8,512]{3,1,2,0:T(8,128)(2,1)S(1)} %get-tuple-element.171, bf16[1,96,8,512]{3,1,2,0:T(8,128)(2,1)S(1)} %get-tuple-element.165, ...), kind=kOutput, calls=%fused_computation.93 | convolution fusion | flops 233736192 | bytes 3987456 | tf_op jit(solution)/shard_map/ok,rkyp->royp/dot_general | solution.py:66
  43.8 1.6 pad_maximum_fusion
  45.4 1.9 %fusion.61 = f32[8,512,96]{1,2,0:T(8,128)} fusion(bf16[96,96]{1,0:T(8,128)(2,1)S(1)} %get-tuple-element.126, bf16[96,96]{1,0:T(8,128)(2,1)S(1)} %get-tuple-element.127, bf16[96,96]{1,0:T(8,128)(2,1)S(1)} %get-tuple-element.128, bf16[1,96,8,512]{3,1,2,0:T(8,128)(2,1)S(1)} %get-tuple-element.178, bf16[1,96,8,512]{3,1,2,0:T(8,128)(2,1)S(1)} %get-tuple-element.169, ...), kind=kOutput, calls=%fused_computation.95 | convolution fusion | flops 233736192 | bytes 3987456 | tf_op jit(solution)/shard_map/ok,rkyp->royp/dot_general | solution.py:66
  47.3 1.9 %fusion.49 = f32[8,512,96]{1,2,0:T(8,128)} fusion(bf16[96,96]{1,0:T(8,128)(2,1)S(1)} %get-tuple-element.108, bf16[96,96]{1,0:T(8,128)(2,1)S(1)} %get-tuple-element.109, bf16[96,96]{1,0:T(8,128)(2,1)S(1)} %get-tuple-element.110, bf16[1,96,8,512]{3,1,2,0:T(8,128)(2,1)S(1)} %get-tuple-element.176, bf16[1,96,8,512]{3,1,2,0:T(8,128)(2,1)S(1)} %get-tuple-element.167, ...), kind=kOutput, calls=%fused_computation.83 | convolution fusion | flops 233736192 | bytes 3987456 | tf_op jit(solution)/shard_map/ok,rkyp->royp/dot_general | solution.py:66
  49.3 0.5 pad_maximum_fusion.6
  49.7 0.7 copy-done.31
  50.4 0.5 copy-done.33
  50.9 0.5 copy-done.34
  51.4 6.0 %convert_reduce_fusion = (f32[96]{0:T(128)S(1)}, bf16[1,96,8,512]{3,1,2,0:T(8,128)(2,1)S(1)}, bf16[1,96,8,512]{3,1,2,0:T(8,128)(2,1)}) fusion(bf16[1,96,8,512]{3,2,1,0:T(8,128)(2,1)S(1)} %copy-done.31, f32[96]{0:T(128)S(1)} %copy-done.32, f32[8,512,96]{1,2,0:T(8,128)} %fusion.45, bf16[1,96,8,512]{3,1,2,0:T(8,128)(2,1)S(1)} %get-tuple-element.170, ...), kind=kOutput, calls=%fused_computation.120 | convolution fusion | flops 247105440 | bytes 17357568 | tf_op jit(solution)/shard_map/ok,rkyp->royp/dot_general | solution.py:66
  57.4 0.8 fusion.228
  58.2 1.6 fusion.88
  59.7 1.3 collective-permute-start.2
  61.0 5.1 %collective-permute-start.3 = (bf16[1,96,2,512]{3,1,2,0:T(8,128)(2,1)}, bf16[1,96,2,512]{3,1,2,0:T(8,128)(2,1)S(1)}, u32[]{:S(2)}, u32[]{:S(2)}) collective-permute-start(bf16[1,96,2,512]{3,1,2,0:T(8,128)(2,1)} %get-tuple-element.63), channel_id=1, source_target_pairs={{0,1},{1,2},{2,3},{4,5},{5,6},{6,7},{8,9},{9,10},{10,11},{12,13},{... | collective-permute-start | bytes 589832 | tf_op jit(solution)/shard_map/ppermute | solution.py:19
  66.1 1.6 fusion.87
  67.7 1.6 fusion.86
  69.2 1.6 fusion.85
  70.8 1.6 fusion.84
  72.4 1.6 fusion.83
  73.9 1.6 fusion.82
  75.5 1.6 fusion.81
  77.0 1.6 fusion.80
  78.6 1.3 copy.40
  79.9 32.9 %psum.15 = f32[96]{0:T(128)S(1)} all-reduce(f32[96]{0:T(128)S(1)} %get-tuple-element.8), channel_id=1, replica_groups=mesh['groups'=2,'dp'=4,'gy'=4] {'dp','gy'}, use_global_device_ids=true, to_apply=%region_3.4 | all-reduce | flops 96 | bytes 768 | tf_op jit(solution)/shard_map/psum | solution.py:98
  112.9 0.6 multiply_reduce_fusion.1
  113.5 1.0 fusion.89
  114.5 1.8 pad_select_fusion
  116.4 0.7 fusion.99
  117.1 1.0 fusion.102
  118.2 1.0 fusion.97
  119.2 2.5 %pad_select_fusion.1 = (bf16[1,96,8,512]{3,1,2,0:T(8,128)(2,1)S(1)}, bf16[1,96,8,512]{3,1,2,0:T(8,128)(2,1)S(1)}, bf16[1,96,8,512]{3,1,2,0:T(8,128)(2,1)S(1)}, b...) fusion(bf16[1,96,8,482]{3,1,2,0:T(8,128)(2,1)S(1)} %get-tuple-e, ...), kind=kLoop, calls=%fused_computation.191 | loop fusion | flops 3538944 | bytes 13852160 | tf_op jit(solution)/shard_map/jit(_where)/select_n | solution.py:37
  121.7 4.0 %fusion.104 = (bf16[1,96,8,512]{3,1,2,0:T(8,128)(2,1)S(1)}, bf16[1,96,8,512]{3,1,2,0:T(8,128)(2,1)S(1)}, bf16[1,96,8,512]{3,1,2,0:T(8,128)(2,1)S(1)}, bf16[1,96,...) fusion(bf16[1,96,8,512]{3,1,2,0:T(8,128)(2,1)S(1)} %get-tuple-e, ...), kind=kLoop, calls=%fused_computation.171 | loop fusion | flops 12976128 | bytes 15923200 | tf_op jit(solution)/shard_map/jit(_where)/select_n | solution.py:37
  125.8 0.7 fusion.30
  126.6 0.7 fusion.25
  127.4 0.7 fusion.15
  128.2 0.7 fusion
  129.0 0.7 fusion.5
  129.8 0.7 fusion.10
  130.6 0.7 fusion.35
  131.4 0.7 fusion.20
  132.1 2.2 %fusion.107 = bf16[1,96,8,512]{3,1,2,0:T(8,128)(2,1)S(1)} fusion(f32[8,512,96]{1,2,0:T(8,128)S(1)} %fusion.35, f32[8,512,96]{1,2,0:T(8,128)S(1)} %fusion.30, f32[8,512,96]{1,2,0:T(8,128)S(1)} %fusion.25, f32[8,512,96]{1,2,0:T(8,128)S(1)} %fusion.20, f32[8,512,96]{1,2,0:T(8,128)S(1)} %fusion.15, f32[8,512,96]{1,2,0:T(8,128)S(1)} %fusion.10, ...), kind=kOutput, calls=%fused_computation.174 | convolution fusion | flops 237275136 | bytes 15783936 | tf_op jit(solution)/shard_map/ok,rkyp->royp/dot_general | solution.py:66
  134.3 1.3 copy.41
  135.7 38.7 %all-reduce.50.cloned.1.call-done = f32[27,96,96]{2,1,0:T(8,128)} async-done(((f32[27,96,96]{2,1,0:T(8,128)}), f32[27,96,96]{2,1,0:T(8,128)}) %all-reduce.50.cloned.1.call-update) | async-done | bytes 995344 | tf_op jit(solution)/shard_map/psum | solution.py:98
  174.3 2.3 %multiply_reduce_fusion = f32[]{:T(128)} fusion(f32[27,96,96]{2,1,0:T(8,128)} %all-reduce.50.cloned.1.call-done), kind=kLoop, calls=%fused_computation.121 | loop fusion | flops 497663 | bytes 995332 | tf_op jit(solution)/shard_map/reduce_sum | solution.py:99
  177.9 0.5 broadcast_multiply_fusion.1
  178.4 2.5 %broadcast_multiply_fusion = f32[27,96,96]{2,1,0:T(8,128)} fusion(f32[27,96,96]{2,1,0:T(8,128)} %all-reduce.50.cloned.1.call-done, f32[]{:T(128)S(6)} %min.3), kind=kLoop, calls=%fused_computation.238 | loop fusion | flops 248832 | bytes 1990660 | tf_op jit(solution)/shard_map/mul | solution.py:101
  (99 shorter events, 5.7 us)
Async XLA Ops:
  7.2 8.9 %copy-start = (bf16[1,96,8,512]{3,2,1,0:T(8,128)(2,1)S(1)}, bf16[1,96,8,512]{3,2,1,0:T(8,128)(2,1)}, u32[]{:S(2)}) copy-start(bf16[1,96,8,512]{3,2,1,0:T(8,128)(2,1)} %param.4) | copy-start | bytes 2359300
  7.2 8.1 %copy-start.2 = (bf16[27,96,96]{2,1,0:T(8,128)(2,1)S(1)}, bf16[27,96,96]{2,1,0:T(8,128)(2,1)}, u32[]{:S(2)}) copy-start(bf16[27,96,96]{2,1,0:T(8,128)(2,1)} %param.5) | copy-start | bytes 1492996
  7.2 167.2 %all-reduce.50.cloned.1.call-start = ((), (), s32[]{:S(2)}) async-start(), calls=%async_computation | async-start | bytes 2654208 | tf_op jit(solution)/shard_map/psum | solution.py:98
  9.1 11.4 %collective-permute-start.1 = (bf16[1,96,2,512]{3,1,2,0:T(8,128)(2,1)S(1)}, bf16[1,96,2,512]{3,1,2,0:T(8,128)(2,1)S(1)}, u32[]{:S(2)}, u32[]{:S(2)}) collective-permute-start(bf16[1,96,2,512]{3,1,2,0:T(8,128)(2,1)S(1)} %copy.73), channel_id=1, source_target_pairs={{1,0},{2,1},{3,2},{5,4},{6,5},{7,6},{9,8},{10,9},{11,10},{13,12},{... | collective-permute-start | bytes 589832 | tf_op jit(solution)/shard_map/ppermute | solution.py:20
  10.4 9.1 %collective-permute-start = (bf16[1,96,2,512]{3,1,2,0:T(8,128)(2,1)S(1)}, bf16[1,96,2,512]{3,1,2,0:T(8,128)(2,1)S(1)}, u32[]{:S(2)}, u32[]{:S(2)}) collective-permute-start(bf16[1,96,2,512]{3,1,2,0:T(8,128)(2,1)S(1)} %copy.82), channel_id=1, source_target_pairs={{0,1},{1,2},{2,3},{4,5},{5,6},{6,7},{8,9},{9,10},{10,11},{12,13},{... | collective-permute-start | bytes 589832 | tf_op jit(solution)/shard_map/ppermute | solution.py:19
  49.3 1.1 copy-start.31
  49.3 1.1 copy-start.32
  49.3 1.7 copy-start.33
  49.3 2.1 %copy-start.34 = (f32[8,512,96]{1,2,0:T(8,128)S(1)}, f32[8,512,96]{1,2,0:T(8,128)}, u32[]{:S(2)}) copy-start(f32[8,512,96]{1,2,0:T(8,128)} %fusion.53) | copy-start | bytes 4718596
  51.4 6.8 %copy-start.1 = (bf16[1,288,8,512]{3,1,2,0:T(8,128)(2,1)S(1)}, bf16[1,288,8,512]{3,1,2,0:T(8,128)(2,1)}, u32[]{:S(2)}) copy-start(bf16[1,288,8,512]{3,1,2,0:T(8,128)(2,1)} %get-tuple-element.181) | copy-start | bytes 7077892
  59.7 53.8 %collective-permute-start.2 = (bf16[1,96,2,512]{3,1,2,0:T(8,128)(2,1)}, bf16[1,96,2,512]{3,1,2,0:T(8,128)(2,1)S(1)}, u32[]{:S(2)}, u32[]{:S(2)}) collective-permute-start(bf16[1,96,2,512]{3,1,2,0:T(8,128)(2,1)} %get-tuple-element.62), channel_id=1, source_target_pairs={{1,0},{2,1},{3,2},{5,4},{6,5},{7,6},{9,8},{10,9},{11,10},{13,12},{... | collective-permute-start | bytes 589832 | tf_op jit(solution)/shard_map/ppermute | solution.py:20
  61.0 52.5 %collective-permute-start.3 = (bf16[1,96,2,512]{3,1,2,0:T(8,128)(2,1)}, bf16[1,96,2,512]{3,1,2,0:T(8,128)(2,1)S(1)}, u32[]{:S(2)}, u32[]{:S(2)}) collective-permute-start(bf16[1,96,2,512]{3,1,2,0:T(8,128)(2,1)} %get-tuple-element.63), channel_id=1, source_target_pairs={{0,1},{1,2},{2,3},{4,5},{5,6},{6,7},{8,9},{9,10},{10,11},{12,13},{... | collective-permute-start | bytes 589832 | tf_op jit(solution)/shard_map/ppermute | solution.py:19
  77.0 1.6 copy-start.3
  121.7 4.1 %copy-start.10 = (bf16[96,96]{0,1:T(8,128)(2,1)S(1)}, bf16[96,96]{0,1:T(8,128)(2,1)}, u32[]{:S(2)}) copy-start(bf16[96,96]{0,1:T(8,128)(2,1)} %get-tuple-element.97) | copy-start | bytes 55300
  121.7 4.1 %copy-start.11 = (bf16[96,96]{0,1:T(8,128)(2,1)S(1)}, bf16[96,96]{0,1:T(8,128)(2,1)}, u32[]{:S(2)}) copy-start(bf16[96,96]{0,1:T(8,128)(2,1)} %get-tuple-element.98) | copy-start | bytes 55300
  121.7 4.1 %copy-start.12 = (bf16[96,96]{0,1:T(8,128)(2,1)S(1)}, bf16[96,96]{0,1:T(8,128)(2,1)}, u32[]{:S(2)}) copy-start(bf16[96,96]{0,1:T(8,128)(2,1)} %get-tuple-element.99) | copy-start | bytes 55300
  125.8 0.8 copy-start.28
  125.8 0.8 copy-start.29
  125.8 0.8 copy-start.30
  126.6 0.8 copy-start.25
  126.6 0.8 copy-start.26
  126.6 0.8 copy-start.27
  127.4 0.8 copy-start.22
  127.4 0.8 copy-start.23
  127.4 0.8 copy-start.24
  128.2 0.8 copy-start.19
  128.2 0.8 copy-start.20
  128.2 0.8 copy-start.21
  129.0 0.8 copy-start.16
  129.0 0.8 copy-start.17
  129.0 0.8 copy-start.18
  129.8 0.8 copy-start.7
  129.8 0.8 copy-start.8
  129.8 0.8 copy-start.9
  130.5 0.8 copy-start.13
  130.6 0.8 copy-start.14
  130.6 0.8 copy-start.15
  131.3 0.8 copy-start.4
  131.3 0.8 copy-start.5
  131.4 0.8 copy-start.6
Sparse Core Ops, SparseCore 0:
  78.7 95.5 all-reduce.49
where the time goes:
time: 189 us; the launch traced here: 188 us
  matrix products  43.4 us (23%)
  waiting for transfers between devices  38.7 us (20%)
  blocking collectives  32.9 us (17%)
  other arithmetic  29.8 us (16%)
  between operations  16.3 us (9%)
  local copies, waits for them, and re-layouts  15.9 us (8%)
  starting transfers between devices  10.7 us (6%)
    psum x1, waiting for transfers between devices, shards(): wsum, bsum = lax.psum((local_kernel, local_bias), ('dp', 'gy'))  38.7 us
    psum x1, blocking collectives, shards(): wsum, bsum = lax.psum((local_kernel, local_bias), ('dp', 'gy'))  32.9 us
    dot_general x18, matrix products, convolve(): jnp.einsum('ok,rkyp->royp', block, patches, preferred_element_type=jnp.fl...  29.4 us
    select_n x6, other arithmetic, shift_cells(): return jnp.where(valid_cells, moved_cells, jnp.zeros((), values.dtype))  15.9 us
    dot_general x9, matrix products, kernel_grads(): jnp.einsum('royp,rkyp->ok', slope, patches, preferred_element_type=jnp.fl...  14 us
    ppermute x2, starting transfers between devices, padded_2(): before = lax.ppermute(last, axis, up)  8.13 us
    unnamed x83, local copies, waits for them, and re-layouts  6.37 us
    concatenate x5, other arithmetic, padded_2(): x = jnp.concatenate([before, x, after], axis=dim)  4.82 us
  transfers between devices with their start and end apart: 5, of which 1 were waited for; matrix products, arithmetic and copies ran while one was open for 23% of the time, Pallas kernels for 0%

commit v1 on v0

v1 whole, which is shorter than its diff:
```python
import functools

import jax
import jax.numpy as jnp
from jax import lax
from jax.experimental import pallas as pl
from jax.experimental.pallas import tpu as pltpu
from jax.sharding import PartitionSpec as P

CZ = 16
clip_norm = 512.0
ROOT = 0.7978845608028654


def to_rows(src_ref, tile_ref, put):
    channels, count, cells = src_ref.shape
    for lane in range(cells // 128):
        part = src_ref[:, :, lane * 128 : lane * 128 + 128].astype(jnp.float32)
        tile_ref[lane, : channels * count, :] = part.reshape(channels * count, 128)
    for row in range(count):
        for lane in range(cells // 128):
            put(row, lane, tile_ref[lane, pl.ds(row, channels, stride=count), :])


def from_rows(dst_ref, tile_ref):
    channels, count, cells = dst_ref.shape
    for lane in range(cells // 128):
        part = tile_ref[lane, : channels * count, :].reshape(channels, count, 128)
        dst_ref[:, :, lane * 128 : lane * 128 + 128] = part.astype(dst_ref.dtype)


def build(row, patch_ref, index):
    channels, cells = row.shape
    place = lax.broadcasted_iota(jnp.int32, (1, cells), 1)
    depth = place % CZ
    wide = row.astype(jnp.float32)
    for tx in range(3):
        for tz in range(3):
            k = 3 * tx + tz
            dx, dz = 2 * (tx - 1), 2 * (tz - 1)
            offset = dx * CZ + dz
            if offset == 0:
                moved = row
            else:
                valid = (depth + dz >= 0) & (depth + dz < CZ)
                valid = valid & (place + dx * CZ >= 0) & (place + dx * CZ < cells)
                moved = pltpu.roll(wide, (-offset) % cells, 1)
                moved = jnp.where(valid, moved, 0.0).astype(jnp.bfloat16)
            patch_ref[index, k * channels : (k + 1) * channels, :] = moved


def convolve_row(weight_ref, patch_ref, acc_ref, padded, first, last):
    channels = acc_ref.shape[1]
    result = jnp.dot(
        weight_ref[first * channels : last * channels, :],
        patch_ref[padded],
        preferred_element_type=jnp.float32,
    )
    for ty in range(first, last):
        part = result[(ty - first) * channels : (ty - first + 1) * channels]
        yield ty, padded - 2 * ty, part


def taps_of(padded, count):
    return [ty for ty in range(3) if 0 <= padded - 2 * ty < count]


def convolve(weight_ref, patch_ref, acc_ref, order):
    count = acc_ref.shape[0]
    seen = set()
    for padded in order:
        tys = taps_of(padded, count)
        for ty, y, part in convolve_row(
            weight_ref, patch_ref, acc_ref, padded, tys[0], tys[-1] + 1
        ):
            if y in seen:
                acc_ref[y] += part
            else:
                acc_ref[y] = part
                seen.add(y)


def gelu_pair(v, upstream):
    square = v * v
    t = jnp.tanh(ROOT * (v + 0.044715 * (v * square)))
    half = 0.5 * (1.0 + t)
    inner = ROOT * (1.0 + 3 * 0.044715 * square)
    return v * half, upstream * (half + 0.5 * v * (1.0 - t * t) * inner)


def forward_kernel(
    f_ref, up_ref, down_ref, w_ref, b_ref, cot_ref, act_ref, s_ref, wg_ref, bs_ref,
    tile_ref, x_ref, patch_ref, acc_ref, cot_rows_ref,
):
    channels, count, cells = f_ref.shape

    def putter(ref, base):
        def put(row, lane, value):
            ref[base + row, :, lane * 128 : lane * 128 + 128] = value.astype(jnp.bfloat16)

        return put

    to_rows(f_ref, tile_ref, putter(x_ref, 2))
    to_rows(up_ref, tile_ref, putter(x_ref, 0))
    to_rows(down_ref, tile_ref, putter(x_ref, count + 2))
    to_rows(cot_ref, tile_ref, putter(cot_rows_ref, 0))
    for padded in range(count + 4):
        build(x_ref[padded], patch_ref, padded)
    convolve(w_ref, patch_ref, acc_ref, range(count + 4))
    bias = b_ref[...]
    total = jnp.zeros((channels, 128), jnp.float32)
    for y in range(count):
        for lane in range(cells // 128):
            cut = slice(lane * 128, lane * 128 + 128)
            act, slope = gelu_pair(
                acc_ref[y, :, cut] + bias, cot_rows_ref[y, :, cut].astype(jnp.float32)
            )
            slope = slope.astype(jnp.bfloat16)
            s_ref[y, :, cut] = slope
            total = total + slope.astype(jnp.float32)
            tile_ref[lane, pl.ds(y, channels, stride=count), :] = act
    from_rows(act_ref, tile_ref)
    bs_ref[...] = total
    wg_ref[...] = jnp.zeros_like(wg_ref)
    for padded in range(count + 4):
        tys = taps_of(padded, count)
        left = jnp.concatenate([s_ref[padded - 2 * ty] for ty in tys], axis=0)
        grads = lax.dot_general(
            left, patch_ref[padded], (((1,), (1,)), ((), ())),
            preferred_element_type=jnp.float32,
        )
        wg_ref[tys[0] * channels : (tys[-1] + 1) * channels, :] += grads


def backward_kernel(s_ref, up_ref, down_ref, w_ref, fg_ref, tile_ref, patch_ref, acc_ref):
    channels, count, cells = fg_ref.shape
    for padded in range(count + 4):
        if padded < 2:
            row = up_ref[padded]
        elif padded < count + 2:
            row = s_ref[padded - 2]
        else:
            row = down_ref[padded - count - 2]
        build(row, patch_ref, padded)
    convolve(w_ref, patch_ref, acc_ref, range(count + 4))
    for y in range(count):
        for lane in range(cells // 128):
            cut = slice(lane * 128, lane * 128 + 128)
            tile_ref[lane, pl.ds(y, channels, stride=count), :] = acc_ref[y, :, cut]
    from_rows(fg_ref, tile_ref)


def halo(first, last, axis):
    count = lax.axis_size(axis)
    up = [(i, (i + 1) % count) for i in range(count - 1)]
    down = [(j, i) for i, j in up]
    return lax.ppermute(last, axis, up), lax.ppermute(first, axis, down)


def shards(fields, kernel_taps, bias_vector, cotangent):
    channels, count, cells = fields.shape[1:]
    x, cot = fields[0], cotangent[0]
    up, down = halo(x[:, :2], x[:, count - 2 :], "gy")
    taps = kernel_taps.reshape(3, 9, channels, channels)
    w_fwd = taps.transpose(0, 2, 1, 3).reshape(3 * channels, 9 * channels)
    w_bwd = taps[::-1, ::-1].transpose(0, 3, 1, 2).reshape(3 * channels, 9 * channels)
    vmem = pl.BlockSpec(memory_space=pltpu.VMEM)
    params = pltpu.CompilerParams(vmem_limit_bytes=56 * 1024 * 1024)
    f32, b16 = jnp.float32, jnp.bfloat16
    tile = pltpu.VMEM((cells // 128, channels * count, 128), f32)
    patch = pltpu.VMEM((count + 4, 9 * channels, cells), b16)
    acc = pltpu.VMEM((count, channels, cells), f32)
    activated, slope, wg, bs = pl.pallas_call(
        forward_kernel,
        out_shape=(
            jax.ShapeDtypeStruct((channels, count, cells), b16),
            jax.ShapeDtypeStruct((count, channels, cells), b16),
            jax.ShapeDtypeStruct((3 * channels, 9 * channels), f32),
            jax.ShapeDtypeStruct((channels, 128), f32),
        ),
        in_specs=[vmem] * 6,
        out_specs=(vmem,) * 4,
        scratch_shapes=[
            tile,
            pltpu.VMEM((count + 4, channels, cells), b16),
            patch,
            acc,
            pltpu.VMEM((count, channels, cells), b16),
        ],
        compiler_params=params,
    )(x, up, down, w_fwd, bias_vector[:, None], cot)
    s_up, s_down = halo(slope[:2], slope[count - 2 :], "gy")
    wsum, bsum = lax.psum((wg, jnp.sum(bs, axis=1)), ("dp", "gy"))
    field_grad = pl.pallas_call(
        backward_kernel,
        out_shape=jax.ShapeDtypeStruct((channels, count, cells), b16),
        in_specs=[vmem] * 4,
        out_specs=vmem,
        scratch_shapes=[tile, patch, acc],
        compiler_params=params,
        cost_estimate=pl.CostEstimate(
            flops=2 * 27 * channels * channels * cells * count,
            bytes_accessed=3000000, transcendentals=0,
        ),
    )(slope, s_up, s_down, w_bwd)
    grad_norm = jnp.sqrt(jnp.sum(wsum * wsum) + jnp.sum(bsum * bsum) + 1e-06)
    factor = jnp.minimum(1.0, clip_norm / grad_norm)
    kernel_grad = (wsum * factor).reshape(3, channels, 9, channels).transpose(0, 2, 1, 3)
    return (
        activated[None],
        field_grad[None],
        kernel_grad.reshape(27, channels, channels),
        bsum * factor,
    )


def solution(mesh):
    in_specs = (
        P(("groups", "dp"), None, "gy", None),
        P(),
        P(),
        P(("groups", "dp"), None, "gy", None),
    )
    out_specs = (
        P(("groups", "dp"), None, "gy", None),
        P(("groups", "dp"), None, "gy", None),
        P("groups", None, None),
        P("groups"),
    )
    return jax.shard_map(shards, mesh=mesh, in_specs=in_specs, out_specs=out_specs, check_vma=False)
```

time: 189 us -> 141 us (0.75)
  matrix products: 43.4 us -> 0 us
  other arithmetic: 29.8 us -> 3.54 us
  Pallas kernels: 0 us -> 17.7 us
  waiting for transfers between devices: 38.7 us -> 42.5 us
  local copies, waits for them, and re-layouts: 15.9 us -> 17.9 us
    dot_general x27 -> x0, matrix products: 43.4 us -> none  [the longest x18 29.4 us: convolve(): jnp.einsum('ok,rkyp->royp', block, patches, preferred_element_type=jnp.fl...]
    pallas_call x0 -> x2, Pallas kernels: none -> 17.7 us  [the longest x1 11.6 us: shards(): pl.pallas_call(forward_kernel, out_shape=(jax.ShapeDtypeStruct((channels,...]
    select_n x6 -> x0, other arithmetic: 15.9 us -> none  [shift_cells(): return jnp.where(valid_cells, moved_cells, jnp.zeros((), values.dtype))]
    concatenate x10 -> x0, other arithmetic: 7.98 us -> none  [the longest x5 4.82 us: padded_2(): x = jnp.concatenate([before, x, after], axis=dim)]
    reshape x0 -> x7, local copies, waits for them, and re-layouts: none -> 6.74 us  [the longest x2 2.51 us: shards(): taps = kernel_taps.reshape(3, 9, channels, channels)]
    unnamed x83 -> x14, local copies, waits for them, and re-layouts: 6.37 us -> 2.09 us
    slice x14 -> x2, local copies, waits for them, and re-layouts: 7.04 us -> 2.97 us  [the longest x1 1.86 us: shards(): up, down = halo(x[:, :2], x[:, count - 2:], 'gy')]
    psum x1, waiting for transfers between devices: 38.7 us -> 42.5 us  [shards(): wsum, bsum = lax.psum((wg, jnp.sum(bs, axis=1)), ('dp', 'gy'))]
  transfers between devices with their start and end apart: 5 -> 5, of which waited for: 1 -> 1; matrix products, arithmetic and copies ran while one was open for 23% -> 8% of each run, Pallas kernels for 0% -> 4%
where the time goes in v1:
time: 141 us
  waiting for transfers between devices  42.5 us (30%)
  blocking collectives  32.7 us (23%)
  local copies, waits for them, and re-layouts  17.9 us (13%)
  Pallas kernels  17.7 us (13%)
  between operations  15.5 us (11%)
  starting transfers between devices  10.8 us (8%)
  other arithmetic  3.54 us (3%)
    psum x1, waiting for transfers between devices, shards(): wsum, bsum = lax.psum((wg, jnp.sum(bs, axis=1)), ('dp', 'gy'))  42.5 us
    psum x1, blocking collectives, shards(): wsum, bsum = lax.psum((wg, jnp.sum(bs, axis=1)), ('dp', 'gy'))  32.7 us
    pallas_call x1, Pallas kernels, shards(): pl.pallas_call(forward_kernel, out_shape=(jax.ShapeDtypeStruct((channels,...  11.6 us
    ppermute x4, starting transfers between devices, halo(): return (lax.ppermute(last, axis, up), lax.ppermute(first, axis, down))  10.7 us
    pallas_call x1, Pallas kernels, shards(): pl.pallas_call(backward_kernel, out_shape=jax.ShapeDtypeStruct((channels,...  6.15 us
    reduce_sum x2, other arithmetic, shards(): grad_norm = jnp.sqrt(jnp.sum(wsum * wsum) + jnp.sum(bsum * bsum) + 1e-06)  2.86 us
  transfers between devices with their start and end apart: 5, of which 1 were waited for; matrix products, arithmetic and copies ran while one was open for 8% of the time, Pallas kernels for 4%

profile of v1, /device:TPU:0, one launch (start us, length us, event | category | flops | bytes accessed | tf_op | source)
XLA Modules:
  0.0 140.6 jit_solution(4574308354493888523)
XLA Ops:
  7.2 0.0 all-reduce.2.cloned.1.call-start
  7.2 1.9 %fusion.1 = (bf16[96,2,512]{2,1,0:T(2,128)(2,1)S(1)}, bf16[96,2,512]{2,1,0:T(2,128)(2,1)S(1)}) fusion(bf16[96,8,512]{2,1,0:T(8,128)(2,1)} %bitcast.21), kind=kLoop, calls=%fused_computation.5 | loop fusion | bytes 786432 | tf_op jit(solution)/shard_map/slice | solution.py:163
  9.1 1.3 collective-permute-start.1
  10.4 3.0 %collective-permute-start = (bf16[96,2,512]{2,1,0:T(2,128)(2,1)S(1)}, bf16[96,2,512]{2,1,0:T(2,128)(2,1)S(1)}, u32[]{:S(2)}, u32[]{:S(2)}) collective-permute-start(bf16[96,2,512]{2,1,0:T(2,128)(2,1)S(1)} %get-tuple-element.15), channel_id=1, source_target_pairs={{0,1},{1,2},{2,3},{4,5},{5,6},{6,7},{8,9},{9,10},{10,11},{12,13},{... | collective-permute-start | bytes 589832 | tf_op jit(solution)/shard_map/ppermute | solution.py:157
  13.4 1.4 copy.20.b_ref
  14.8 2.0 %copy.18 = bf16[3,9,96,96]{2,0,3,1:T(4,128)(2,1)S(1)} copy(bf16[3,9,96,96]{3,2,1,0:T(8,128)(2,1)} %bitcast.19) | data formatting | bytes 995328 | tf_op jit(solution)/shard_map/reshape | solution.py:164
  16.8 0.6 reshape.24
  17.4 1.1 copy.19.w_ref
  18.5 0.0 collective-permute-done.1.down_ref
  18.5 0.0 copy-start.2
  18.5 0.0 collective-permute-done.up_ref
  18.5 0.0 copy-start.3
  18.5 0.7 copy-done.2
  19.2 0.1 copy-done.3
  19.3 11.6 %shard_map.75 = (bf16[96,8,512]{2,1,0:T(8,128)(2,1)}, bf16[8,96,512]{2,1,0:T(8,128)(2,1)}, f32[288,864]{1,0:T(8,128)}, f32[96,128]{1,0:T(8,128)}) custom-call(bf16[96,8,512]{2,1,0:T(8,128)(2,1)} %bitcast.22, bf16[96,2,512]{2,1,0:T(2,128)(2,1)} %copy-done.3, bf16[96,2,512]{2,1,0:T(2,128)(2,1)} %copy-done.2, bf16[288,864]{1,0:T(8,128)(2,1)} %copy.19.w_ref, ...), custom_call_target="tpu_custom_call" | custom-call | tf_op jit(solution)/shard_map/pallas_call | solution.py:173
  30.9 0.0 copy-start.1
  30.9 0.0 all-reduce.2.cloned.1.call-update
  30.9 1.1 fusion
  32.0 1.3 collective-permute-start.3
  33.3 5.1 %collective-permute-start.2 = (bf16[2,96,512]{2,1,0:T(8,128)(2,1)S(1)}, bf16[2,96,512]{2,1,0:T(8,128)(2,1)S(1)}, u32[]{:S(2)}, u32[]{:S(2)}) collective-permute-start(bf16[2,96,512]{2,1,0:T(8,128)(2,1)S(1)} %get-tuple-element.13), channel_id=1, source_target_pairs={{0,1},{1,2},{2,3},{4,5},{5,6},{6,7},{8,9},{9,10},{10,11},{12,13},{... | collective-permute-start | bytes 589832 | tf_op jit(solution)/shard_map/ppermute | solution.py:157
  38.4 0.0 copy-done.1
  38.4 0.5 copy.21
  38.9 2.4 %rev.3 = bf16[3,9,96,96]{3,0,2,1:T(4,128)(2,1)S(1)} reverse(bf16[3,9,96,96]{3,0,2,1:T(4,128)(2,1)S(1)} %copy.21), dimensions={0,1} | reverse | bytes 995328 | tf_op jit(solution)/shard_map/rev | solution.py:166
  41.2 0.0 copy-start.4
  41.3 0.6 reshape.25
  41.9 1.1 copy.22.w_ref
  42.9 0.0 copy-done.4
  42.9 0.1 reduce_sum.28
  43.1 32.7 %psum.15 = f32[96]{0:T(128)S(1)} all-reduce(f32[96]{0:T(128)S(1)} %reduce_sum.28), channel_id=1, replica_groups=mesh['groups'=2,'dp'=4,'gy'=4] {'dp','gy'}, use_global_device_ids=true, to_apply=%region_3.0 | all-reduce | flops 96 | bytes 768 | tf_op jit(solution)/shard_map/psum | solution.py:193
  75.7 0.7 multiply_reduce_fusion.1
  76.4 0.0 collective-permute-done.3.down_ref
  76.4 0.0 copy-start.5
  76.4 0.0 collective-permute-done.2.up_ref
  76.4 0.7 copy-done.5
  77.1 0.0 copy-start.6
  77.1 0.7 copy-done.6
  77.8 6.1 %shard_map.76 = bf16[96,8,512]{2,1,0:T(8,128)(2,1)} custom-call(bf16[8,96,512]{2,1,0:T(8,128)(2,1)} %get-tuple-element.9.s_ref, bf16[2,96,512]{2,1,0:T(8,128)(2,1)} %copy-done.6, bf16[2,96,512]{2,1,0:T(8,128)(2,1)} %copy-done.5, bf16[288,864]{1,0:T(8,128)(2,1)} %copy.22.w_ref), custom_call_target="tpu_custom_call" | custom-call | flops 2038431744 | bytes 3000000 | tf_op jit(solution)/shard_map/pallas_call | solution.py:194
  83.9 42.5 %all-reduce.2.cloned.1.call-done = f32[288,864]{1,0:T(8,128)} async-done(((f32[288,864]{1,0:T(8,128)}), f32[288,864]{1,0:T(8,128)}) %all-reduce.2.cloned.1.call-update) | async-done | bytes 995344 | tf_op jit(solution)/shard_map/psum | solution.py:193
  126.4 0.0 copy-start
  126.4 2.2 %multiply_reduce_fusion = f32[]{:T(128)} fusion(f32[288,864]{1,0:T(8,128)} %all-reduce.2.cloned.1.call-done), kind=kLoop, calls=%fused_computation | loop fusion | flops 497663 | bytes 995332 | tf_op jit(solution)/shard_map/reduce_sum | solution.py:206
  129.9 0.5 broadcast_multiply_fusion.1
  130.5 0.0 copy-done
  130.5 0.1 broadcast_multiply_fusion
  130.5 0.4 copy.23
  131.0 0.9 reshape.26
  131.9 1.9 %copy.24 = f32[3,9,96,96]{3,2,1,0:T(8,128)} copy(f32[3,9,96,96]{2,0,3,1:T(4,128)S(1)} %bitcast.16) | data formatting | bytes 1990656 | tf_op jit(solution)/shard_map/transpose | solution.py:208
Async XLA Ops:
  7.2 119.2 %all-reduce.2.cloned.1.call-start = ((), (), s32[]{:S(2)}) async-start(), calls=%async_computation | async-start | bytes 2064384 | tf_op jit(solution)/shard_map/psum | solution.py:193
  9.1 9.4 %collective-permute-start.1 = (bf16[96,2,512]{2,1,0:T(2,128)(2,1)S(1)}, bf16[96,2,512]{2,1,0:T(2,128)(2,1)S(1)}, u32[]{:S(2)}, u32[]{:S(2)}) collective-permute-start(bf16[96,2,512]{2,1,0:T(2,128)(2,1)S(1)} %get-tuple-element.14), channel_id=1, source_target_pairs={{1,0},{2,1},{3,2},{5,4},{6,5},{7,6},{9,8},{10,9},{11,10},{13,12},{... | collective-permute-start | bytes 589832 | tf_op jit(solution)/shard_map/ppermute | solution.py:157
  10.4 8.1 %collective-permute-start = (bf16[96,2,512]{2,1,0:T(2,128)(2,1)S(1)}, bf16[96,2,512]{2,1,0:T(2,128)(2,1)S(1)}, u32[]{:S(2)}, u32[]{:S(2)}) collective-permute-start(bf16[96,2,512]{2,1,0:T(2,128)(2,1)S(1)} %get-tuple-element.15), channel_id=1, source_target_pairs={{0,1},{1,2},{2,3},{4,5},{5,6},{6,7},{8,9},{9,10},{10,11},{12,13},{... | collective-permute-start | bytes 589832 | tf_op jit(solution)/shard_map/ppermute | solution.py:157
  18.5 0.7 copy-start.2
  18.5 0.8 copy-start.3
  30.9 7.5 %copy-start.1 = (bf16[27,96,96]{2,1,0:T(8,128)(2,1)S(1)}, bf16[27,96,96]{2,1,0:T(8,128)(2,1)}, u32[]{:S(2)}) copy-start(bf16[27,96,96]{2,1,0:T(8,128)(2,1)} %param.5) | copy-start | bytes 1492996
  32.0 44.4 %collective-permute-start.3 = (bf16[2,96,512]{2,1,0:T(8,128)(2,1)S(1)}, bf16[2,96,512]{2,1,0:T(8,128)(2,1)S(1)}, u32[]{:S(2)}, u32[]{:S(2)}) collective-permute-start(bf16[2,96,512]{2,1,0:T(8,128)(2,1)S(1)} %get-tuple-element.12), channel_id=1, source_target_pairs={{1,0},{2,1},{3,2},{5,4},{6,5},{7,6},{9,8},{10,9},{11,10},{13,12},{... | collective-permute-start | bytes 589832 | tf_op jit(solution)/shard_map/ppermute | solution.py:157
  33.3 43.1 %collective-permute-start.2 = (bf16[2,96,512]{2,1,0:T(8,128)(2,1)S(1)}, bf16[2,96,512]{2,1,0:T(8,128)(2,1)S(1)}, u32[]{:S(2)}, u32[]{:S(2)}) collective-permute-start(bf16[2,96,512]{2,1,0:T(8,128)(2,1)S(1)} %get-tuple-element.13), channel_id=1, source_target_pairs={{0,1},{1,2},{2,3},{4,5},{5,6},{6,7},{8,9},{9,10},{10,11},{12,13},{... | collective-permute-start | bytes 589832 | tf_op jit(solution)/shard_map/ppermute | solution.py:157
  41.2 1.7 %copy-start.4 = (f32[96,128]{1,0:T(8,128)S(1)}, f32[96,128]{1,0:T(8,128)}, u32[]{:S(2)}) copy-start(f32[96,128]{1,0:T(8,128)} %get-tuple-element.11) | copy-start | bytes 147460
  76.4 0.7 copy-start.5
  77.1 0.7 copy-start.6
  126.4 4.1 %copy-start = (f32[288,864]{1,0:T(8,128)S(1)}, f32[288,864]{1,0:T(8,128)}, u32[]{:S(2)}) copy-start(f32[288,864]{1,0:T(8,128)} %all-reduce.2.cloned.1.call-done) | copy-start | bytes 2985988
Sparse Core Ops, SparseCore 0:
  31.0 95.3 all-reduce.1

commit v2 on v1

v2 whole, which is shorter than its diff:
```python
import jax
import jax.numpy as jnp
from jax import lax
from jax.experimental import pallas as pl
from jax.experimental.pallas import tpu as pltpu
from jax.sharding import PartitionSpec as P

CZ = 16
clip_norm = 512.0
ROOT = 0.7978845608028654


def to_rows(src_ref, tile_ref, put):
    channels, count, cells = src_ref.shape
    for lane in range(cells // 128):
        part = src_ref[:, :, lane * 128 : lane * 128 + 128].astype(jnp.float32)
        tile_ref[lane, : channels * count, :] = part.reshape(channels * count, 128)
    for row in range(count):
        for lane in range(cells // 128):
            put(row, lane, tile_ref[lane, pl.ds(row, channels, stride=count), :])


def from_rows(dst_ref, tile_ref):
    channels, count, cells = dst_ref.shape
    for lane in range(cells // 128):
        part = tile_ref[lane, : channels * count, :].reshape(channels, count, 128)
        dst_ref[:, :, lane * 128 : lane * 128 + 128] = part.astype(dst_ref.dtype)


def build(row, patch_ref, index):
    channels, cells = row.shape
    place = lax.broadcasted_iota(jnp.int32, (1, cells), 1)
    depth = place % CZ
    wide = row.astype(jnp.float32)
    for tx in range(3):
        for tz in range(3):
            k = 3 * tx + tz
            dx, dz = 2 * (tx - 1), 2 * (tz - 1)
            offset = dx * CZ + dz
            if offset == 0:
                moved = row
            else:
                valid = (depth + dz >= 0) & (depth + dz < CZ)
                valid = valid & (place + dx * CZ >= 0) & (place + dx * CZ < cells)
                moved = pltpu.roll(wide, (-offset) % cells, 1)
                moved = jnp.where(valid, moved, 0.0).astype(jnp.bfloat16)
            patch_ref[index, k * channels : (k + 1) * channels, :] = moved


def convolve_row(weight_ref, patch_ref, acc_ref, padded, first, last):
    channels = acc_ref.shape[1]
    result = jnp.dot(
        weight_ref[first * channels : last * channels, :],
        patch_ref[padded],
        preferred_element_type=jnp.float32,
    )
    for ty in range(first, last):
        part = result[(ty - first) * channels : (ty - first + 1) * channels]
        yield ty, padded - 2 * ty, part


def taps_of(padded, count):
    return [ty for ty in range(3) if 0 <= padded - 2 * ty < count]


def convolve(weight_ref, patch_ref, acc_ref, order, seen):
    count = acc_ref.shape[0]
    for padded in order:
        tys = taps_of(padded, count)
        for ty, y, part in convolve_row(
            weight_ref, patch_ref, acc_ref, padded, tys[0], tys[-1] + 1
        ):
            if y in seen:
                acc_ref[y] += part
            else:
                acc_ref[y] = part
                seen.add(y)


def gelu_pair(v, upstream):
    square = v * v
    t = jnp.tanh(ROOT * (v + 0.044715 * (v * square)))
    half = 0.5 * (1.0 + t)
    inner = ROOT * (1.0 + 3 * 0.044715 * square)
    return v * half, upstream * (half + 0.5 * v * (1.0 - t * t) * inner)


MESH = pl.DeviceIdType.MESH


def greet(axis):
    me, size = lax.axis_index(axis), lax.axis_size(axis)
    barrier = pltpu.get_barrier_semaphore()
    for peer in (lax.rem(me + size - 1, size), lax.rem(me + 1, size)):
        pl.semaphore_signal(barrier, inc=1, device_id={axis: peer}, device_id_type=MESH)
    pl.semaphore_wait(barrier, 2)


def halo(axis, first, last, before, after, sems):
    me, size = lax.axis_index(axis), lax.axis_size(axis)

    def up():
        return pltpu.make_async_remote_copy(
            src_ref=last, dst_ref=before, send_sem=sems.at[0], recv_sem=sems.at[1],
            device_id={axis: lax.rem(me + 1, size)}, device_id_type=MESH,
        )

    def down():
        return pltpu.make_async_remote_copy(
            src_ref=first, dst_ref=after, send_sem=sems.at[2], recv_sem=sems.at[3],
            device_id={axis: lax.rem(me + size - 1, size)}, device_id_type=MESH,
        )

    def start():
        @pl.when(me < size - 1)
        def _():
            up().start()

        @pl.when(me > 0)
        def _():
            down().start()

    def finish():
        @pl.when(me > 0)
        def _():
            up().wait_recv()
            down().wait_send()

        @pl.when(me == 0)
        def _():
            before[...] = jnp.zeros(before.shape, before.dtype)

        @pl.when(me < size - 1)
        def _():
            down().wait_recv()
            up().wait_send()

        @pl.when(me == size - 1)
        def _():
            after[...] = jnp.zeros(after.shape, after.dtype)

    return start, finish


def forward_kernel(
    f_ref, w_ref, b_ref, cot_ref, act_ref, s_ref, sums_ref,
    tile_ref, x_ref, before_ref, after_ref, patch_ref, acc_ref, cot_rows_ref, wg_ref, sems,
):
    channels, count, cells = f_ref.shape

    def putter(ref):
        def put(row, lane, value):
            ref[row, :, lane * 128 : lane * 128 + 128] = value.astype(jnp.bfloat16)

        return put

    greet("gy")
    to_rows(f_ref, tile_ref, putter(x_ref))
    start, finish = halo(
        "gy", x_ref.at[pl.ds(0, 2)], x_ref.at[pl.ds(count - 2, 2)], before_ref, after_ref, sems
    )
    start()
    to_rows(cot_ref, tile_ref, putter(cot_rows_ref))
    seen = set()
    for padded in range(2, count + 2):
        build(x_ref[padded - 2], patch_ref, padded)
    convolve(w_ref, patch_ref, acc_ref, range(2, count + 2), seen)
    finish()
    for row in range(2):
        build(before_ref[row], patch_ref, row)
        build(after_ref[row], patch_ref, count + 2 + row)
    convolve(w_ref, patch_ref, acc_ref, (0, 1, count + 2, count + 3), seen)
    bias = b_ref[...]
    total = jnp.zeros((channels, 128), jnp.float32)
    for y in range(count):
        for lane in range(cells // 128):
            cut = slice(lane * 128, lane * 128 + 128)
            act, slope = gelu_pair(
                acc_ref[y, :, cut] + bias, cot_rows_ref[y, :, cut].astype(jnp.float32)
            )
            slope = slope.astype(jnp.bfloat16)
            s_ref[y, :, cut] = slope
            total = total + slope.astype(jnp.float32)
            tile_ref[lane, pl.ds(y, channels, stride=count), :] = act
    from_rows(act_ref, tile_ref)
    wg_ref[...] = jnp.zeros_like(wg_ref)
    for padded in range(count + 4):
        tys = taps_of(padded, count)
        left = jnp.concatenate([s_ref[padded - 2 * ty] for ty in tys], axis=0)
        grads = lax.dot_general(
            left, patch_ref[padded], (((1,), (1,)), ((), ())),
            preferred_element_type=jnp.float32,
        )
        wg_ref[tys[0] * channels : (tys[-1] + 1) * channels, : 9 * channels] += grads
    height = 3 * channels
    for lane in range(wg_ref.shape[1] // 128):
        sums_ref[lane * height : (lane + 1) * height, :] = wg_ref[
            :, lane * 128 : lane * 128 + 128
        ].astype(jnp.bfloat16)
    square = jnp.concatenate([total, jnp.zeros((128 - channels, 128), jnp.float32)], axis=0)
    bias_row = jnp.sum(square.T, axis=0, keepdims=True)
    high = bias_row.astype(jnp.bfloat16).astype(jnp.float32)
    used = wg_ref.shape[1] // 128 * height
    index = lax.broadcasted_iota(jnp.int32, (sums_ref.shape[0] - used, 128), 0)
    rest = jnp.where(index == 0, high, jnp.where(index == 1, bias_row - high, 0.0))
    sums_ref[used:, :] = rest.astype(jnp.bfloat16)


def backward_kernel(
    s_ref, w_ref, sums_ref, fg_ref, kg_ref, bg_ref,
    tile_ref, patch_ref, acc_ref, before_ref, after_ref, land1_ref, land2_ref, part_ref, red_ref,
    sems, sends, recvs,
):
    channels, count, cells = fg_ref.shape
    outer, inner = lax.axis_size("gy"), lax.axis_size("dp")
    me_out, me_in = lax.axis_index("gy"), lax.axis_index("dp")
    rows1 = sums_ref.shape[0] // outer
    rows2 = rows1 // inner
    barrier = pltpu.get_barrier_semaphore()
    for axis, me, size in (("gy", me_out, outer), ("dp", me_in, inner)):
        for k in range(1, size):
            pl.semaphore_signal(
                barrier, inc=1, device_id={axis: lax.rem(me + k, size)}, device_id_type=MESH
            )
    pl.semaphore_wait(barrier, outer + inner - 2)

    def spread(axis, me, size, base, source, target):
        copies = []
        for k in range(1, size):
            peer = lax.rem(me + k, size)
            copies.append(
                pltpu.make_async_remote_copy(
                    src_ref=source(peer), dst_ref=target(k),
                    send_sem=sends.at[base + k], recv_sem=recvs.at[base + k],
                    device_id={axis: peer}, device_id_type=MESH,
                )
            )
        for copy in copies:
            copy.start()
        return copies

    def piece(ref, index, length):
        return ref.at[pl.ds(pl.multiple_of(index * length, length), length)]

    start, finish = halo(
        "gy", s_ref.at[pl.ds(0, 2)], s_ref.at[pl.ds(count - 2, 2)], before_ref, after_ref, sems
    )
    start()
    first = spread(
        "gy", me_out, outer, 0,
        lambda peer: piece(sums_ref, peer, rows1), lambda k: land1_ref.at[k - 1],
    )
    for padded in range(2, count + 2):
        build(s_ref[padded - 2], patch_ref, padded)
    seen = set()
    convolve(w_ref, patch_ref, acc_ref, range(2, count + 2), seen)
    for copy in first:
        copy.wait()
    total = piece(sums_ref, me_out, rows1)[...].astype(jnp.float32)
    for k in range(outer - 1):
        total = total + land1_ref[k].astype(jnp.float32)
    part_ref[...] = total.astype(jnp.bfloat16)
    second = spread(
        "dp", me_in, inner, outer,
        lambda peer: piece(part_ref, peer, rows2), lambda k: land2_ref.at[k - 1],
    )
    finish()
    for row in range(2):
        build(before_ref[row], patch_ref, row)
        build(after_ref[row], patch_ref, count + 2 + row)
    for copy in second:
        copy.wait()
    total = piece(part_ref, me_in, rows2)[...].astype(jnp.float32)
    for k in range(inner - 1):
        total = total + land2_ref[k].astype(jnp.float32)
    mine = piece(red_ref, me_out * inner + me_in, rows2)
    mine[...] = total.astype(jnp.bfloat16)
    third = spread("dp", me_in, inner, outer + inner, lambda peer: mine, lambda k: mine)
    convolve(w_ref, patch_ref, acc_ref, (0, 1, count + 2, count + 3), seen)
    for copy in third:
        copy.wait()
    block = piece(red_ref, me_out, rows1)
    fourth = spread("gy", me_out, outer, outer + 2 * inner, lambda peer: block, lambda k: block)
    for y in range(count):
        for lane in range(cells // 128):
            cut = slice(lane * 128, lane * 128 + 128)
            tile_ref[lane, pl.ds(y, channels, stride=count), :] = acc_ref[y, :, cut]
    from_rows(fg_ref, tile_ref)
    for copy in fourth:
        copy.wait()
    height = 3 * channels
    lanes = -(-9 * channels // 128)
    squares = jnp.zeros((height, 128), jnp.float32)
    for lane in range(lanes):
        value = red_ref[lane * height : (lane + 1) * height, :].astype(jnp.float32)
        squares = squares + value * value
    rest = red_ref[lanes * height : lanes * height + 32, :].astype(jnp.float32)
    bias_row = jnp.sum(rest, axis=0, keepdims=True)
    norm = jnp.sum(squares, axis=0, keepdims=True) + bias_row * bias_row
    norm = jnp.sqrt(jnp.sum(norm, axis=1, keepdims=True) + 1e-06)
    factor = jnp.minimum(1.0, clip_norm / norm)
    bg_ref[...] = bias_row * factor
    for ty in range(3):
        wide = jnp.concatenate(
            [
                red_ref[lane * height + ty * channels : lane * height + (ty + 1) * channels, :]
                .astype(jnp.float32)
                for lane in range(lanes)
            ],
            axis=1,
        ) * factor
        for k in range(9):
            kg_ref[9 * ty + k] = wide[:, k * channels : (k + 1) * channels]


def shards(fields, kernel_taps, bias_vector, cotangent):
    channels, count, cells = fields.shape[1:]
    x, cot = fields[0], cotangent[0]
    outer, inner = lax.axis_size("gy"), lax.axis_size("dp")
    taps = kernel_taps.reshape(3, 9, channels, channels)
    w_fwd = taps.transpose(0, 2, 1, 3).reshape(3 * channels, 9 * channels)
    w_bwd = taps[::-1, ::-1].transpose(0, 3, 1, 2).reshape(3 * channels, 9 * channels)
    vmem = pl.BlockSpec(memory_space=pltpu.VMEM)
    f32, b16 = jnp.float32, jnp.bfloat16
    tile = pltpu.VMEM((cells // 128, channels * count, 128), f32)
    patch = pltpu.VMEM((count + 4, 9 * channels, cells), b16)
    acc = pltpu.VMEM((count, channels, cells), f32)
    rows = pltpu.VMEM((count, channels, cells), b16)
    edge = pltpu.VMEM((2, channels, cells), b16)
    lanes = -(-9 * channels // 128)
    unit = 16 * outer * inner
    length = -(-(lanes * 3 * channels + 32) // unit) * unit
    rows1 = length // outer
    rows2 = rows1 // inner
    flops = 2 * 27 * channels * channels * cells * count

    def params(number):
        return pltpu.CompilerParams(
            vmem_limit_bytes=56 * 1024 * 1024, collective_id=number, has_side_effects=True
        )

    activated, slope, sums = pl.pallas_call(
        forward_kernel,
        out_shape=(
            jax.ShapeDtypeStruct((channels, count, cells), b16),
            jax.ShapeDtypeStruct((count, channels, cells), b16),
            jax.ShapeDtypeStruct((length, 128), b16),
        ),
        in_specs=[vmem] * 4,
        out_specs=(vmem,) * 3,
        scratch_shapes=[
            tile, rows, edge, edge, patch, acc, rows,
            pltpu.VMEM((3 * channels, lanes * 128), f32),
            pltpu.SemaphoreType.DMA((4,)),
        ],
        compiler_params=params(0),
        cost_estimate=pl.CostEstimate(
            flops=2 * flops, bytes_accessed=4000000, transcendentals=0
        ),
    )(x, w_fwd, bias_vector[:, None], cot)
    field_grad, kernel_grad, bias_row = pl.pallas_call(
        backward_kernel,
        out_shape=(
            jax.ShapeDtypeStruct((channels, count, cells), b16),
            jax.ShapeDtypeStruct((27, channels, channels), f32),
            jax.ShapeDtypeStruct((1, 128), f32),
        ),
        in_specs=[vmem] * 3,
        out_specs=(vmem,) * 3,
        scratch_shapes=[
            tile, patch, acc, edge, edge,
            pltpu.VMEM((outer - 1, rows1, 128), b16),
            pltpu.VMEM((inner - 1, rows2, 128), b16),
            pltpu.VMEM((rows1, 128), b16),
            pltpu.VMEM((length, 128), b16),
            pltpu.SemaphoreType.DMA((4,)),
            pltpu.SemaphoreType.DMA((2 * (outer + inner),)),
            pltpu.SemaphoreType.DMA((2 * (outer + inner),)),
        ],
        compiler_params=params(1),
        cost_estimate=pl.CostEstimate(flops=flops, bytes_accessed=4000000, transcendentals=0),
    )(slope, w_bwd, sums)
    return activated[None], field_grad[None], kernel_grad, bias_row[0, :channels]


def solution(mesh):
    in_specs = (
        P(("groups", "dp"), None, "gy", None),
        P(),
        P(),
        P(("groups", "dp"), None, "gy", None),
    )
    out_specs = (
        P(("groups", "dp"), None, "gy", None),
        P(("groups", "dp"), None, "gy", None),
        P("groups", None, None),
        P("groups"),
    )
    return jax.shard_map(shards, mesh=mesh, in_specs=in_specs, out_specs=out_specs, check_vma=False)
```

time: 141 us -> 61 us (0.43)
  waiting for transfers between devices: 42.5 us -> 0 us
  blocking collectives: 32.7 us -> 0 us
  Pallas kernels: 17.7 us -> 45.3 us
  between operations: 15.5 us -> 0.71 us
  starting transfers between devices: 10.8 us -> 0 us
  local copies, waits for them, and re-layouts: 17.9 us -> 13.9 us
  other arithmetic: 3.54 us -> 0 us
    psum x1 -> x0, waiting for transfers between devices: 42.5 us -> none  [shards(): wsum, bsum = lax.psum((wg, jnp.sum(bs, axis=1)), ('dp', 'gy'))]
    psum x1 -> x0, blocking collectives: 32.7 us -> none  [shards(): wsum, bsum = lax.psum((wg, jnp.sum(bs, axis=1)), ('dp', 'gy'))]
    pallas_call x1, Pallas kernels: 6.15 us -> 30.5 us  [shards(): pl.pallas_call(backward_kernel, out_shape=(jax.ShapeDtypeStruct((channels...]
    ppermute x4 -> x0, starting transfers between devices: 10.7 us -> none  [halo(): return (lax.ppermute(last, axis, up), lax.ppermute(first, axis, down))]
    pallas_call x1, Pallas kernels: 11.6 us -> 14.8 us  [shards(): pl.pallas_call(forward_kernel, out_shape=(jax.ShapeDtypeStruct((channels,...]
    slice x2 -> x0, local copies, waits for them, and re-layouts: 2.97 us -> none  [the longest x1 1.86 us: shards(): up, down = halo(x[:, :2], x[:, count - 2:], 'gy')]
    reduce_sum x3 -> x0, other arithmetic: 2.96 us -> none  [the longest x2 2.86 us: shards(): grad_norm = jnp.sqrt(jnp.sum(wsum * wsum) + jnp.sum(bsum * bsum) + 1e-06)]
    transpose x1 -> x0, local copies, waits for them, and re-layouts: 1.93 us -> none  [shards(): (wsum * factor).reshape(3, channels, 9, channels).transpose(0, 2, 1, 3)]
  transfers between devices with their start and end apart: 5 -> 0, of which waited for: 1 -> 0; matrix products, arithmetic and copies ran while one was open for 8% -> 0% of each run, Pallas kernels for 4% -> 0%
where the time goes in v2:
time: 61 us; the launch traced here: 59.9 us
  Pallas kernels  45.3 us (74%)
  local copies, waits for them, and re-layouts  13.9 us (23%)
  between operations  0.71 us (1%)
    pallas_call x1, Pallas kernels, shards(): pl.pallas_call(backward_kernel, out_shape=(jax.ShapeDtypeStruct((channels...  30.5 us
    pallas_call x1, Pallas kernels, shards(): pl.pallas_call(forward_kernel, out_shape=(jax.ShapeDtypeStruct((channels,...  14.8 us
    reshape x2, local copies, waits for them, and re-layouts, shards(): taps = kernel_taps.reshape(3, 9, channels, channels)  2.86 us
    unnamed x11, local copies, waits for them, and re-layouts  2.84 us
    rev x1, local copies, waits for them, and re-layouts, shards(): taps[::-1, ::-1].transpose(0, 3, 1, 2).reshape(3 * channels, 9 * channels)  2.37 us
    reshape x2, local copies, waits for them, and re-layouts, shards(): taps[::-1, ::-1].transpose(0, 3, 1, 2).reshape(3 * channels, 9 * channels)  1.65 us
    reshape x2, local copies, waits for them, and re-layouts, shards(): w_fwd = taps.transpose(0, 2, 1, 3).reshape(3 * channels, 9 * channels)  1.65 us
    broadcast_in_dim x1, local copies, waits for them, and re-layouts, shards(): bias_vector[:, None]  1.37 us

profile of v2, /device:TPU:0, one launch (start us, length us, event | category | flops | bytes accessed | tf_op | source)
XLA Modules:
  0.0 59.9 jit_solution(15311448236911825930)
XLA Ops:
  0.6 1.4 %copy.13.b_ref = f32[96,1]{1,0:T(8,128)} copy(f32[96,1]{0,1:T(1,128)} %bitcast.20) | data formatting | bytes 768 | tf_op jit(solution)/shard_map/broadcast_in_dim | solution.py:360
  2.0 1.5 %copy.14 = bf16[3,9,96,96]{3,0,2,1:T(4,128)(2,1)S(1)} copy(bf16[3,9,96,96]{3,2,1,0:T(8,128)(2,1)} %bitcast.16) | data formatting | bytes 995328 | tf_op jit(solution)/shard_map/reshape | solution.py:320
  3.6 2.4 %rev.3 = bf16[3,9,96,96]{3,0,2,1:T(4,128)(2,1)S(1)} reverse(bf16[3,9,96,96]{3,0,2,1:T(4,128)(2,1)S(1)} %copy.14), dimensions={0,1} | reverse | bytes 995328 | tf_op jit(solution)/shard_map/rev | solution.py:322
  5.9 0.0 copy-start
  5.9 0.6 %reshape.19 = bf16[288,864]{0,1:T(8,128)(2,1)S(1)} reshape(bf16[3,96,9,96]{1,0,3,2:T(4,128)(2,1)S(1)} %bitcast.14) | data formatting | bytes 995328 | tf_op jit(solution)/shard_map/reshape | solution.py:322
  6.5 1.1 %copy.15.w_ref = bf16[288,864]{1,0:T(8,128)(2,1)} copy(bf16[288,864]{0,1:T(8,128)(2,1)S(1)} %reshape.19) | data formatting | bytes 995328 | tf_op jit(solution)/shard_map/reshape | solution.py:322
  7.6 0.0 copy-done
  7.6 1.3 %copy.11 = bf16[3,9,96,96]{2,0,3,1:T(4,128)(2,1)S(1)} copy(bf16[3,9,96,96]{3,2,1,0:T(8,128)(2,1)S(1)} %bitcast.17) | data formatting | bytes 995328 | tf_op jit(solution)/shard_map/reshape | solution.py:320
  8.9 0.6 %reshape.18 = bf16[288,864]{0,1:T(8,128)(2,1)S(1)} reshape(bf16[3,96,9,96]{1,0,3,2:T(4,128)(2,1)S(1)} %bitcast.15) | data formatting | bytes 995328 | tf_op jit(solution)/shard_map/reshape | solution.py:321
  9.5 1.1 %copy.12.w_ref = bf16[288,864]{1,0:T(8,128)(2,1)} copy(bf16[288,864]{0,1:T(8,128)(2,1)S(1)} %reshape.18) | data formatting | bytes 995328 | tf_op jit(solution)/shard_map/reshape | solution.py:321
  10.6 14.8 %shard_map.75 = (bf16[96,8,512]{2,1,0:T(8,128)(2,1)}, bf16[8,96,512]{2,1,0:T(8,128)(2,1)}, bf16[2048,128]{1,0:T(8,128)(2,1)}) custom-call(bf16[96,8,512]{2,1,0:T(8,128)(2,1)} %bitcast.21, bf16[288,864]{1,0:T(8,128)(2,1)} %copy.12.w_ref, f32[96,1]{1,0:T(8,128)} %copy.13.b_ref, bf16[96,8,512]{2,1,0:T(8,128)(2,1)} %bitcast.22), custom_call_target="tpu_custom_call" | custom-call | flops 4076863488 | bytes 4000000 | tf_op jit(solution)/shard_map/pallas_call | solution.py:342
  25.4 0.0 copy-start.2
  25.4 30.5 %shard_map.76 = (bf16[96,8,512]{2,1,0:T(8,128)(2,1)}, f32[27,96,96]{2,1,0:T(8,128)}, f32[1,128]{1,0:T(1,128)}) custom-call(bf16[8,96,512]{2,1,0:T(8,128)(2,1)} %get-tuple-element.11.s_ref, bf16[288,864]{1,0:T(8,128)(2,1)} %copy.15.w_ref, bf16[2048,128]{1,0:T(8,128)(2,1)} %get-tuple-element.12.sums_ref), custom_call_target="tpu_custom_call" | custom-call | flops 2038431744 | bytes 4000000 | tf_op jit(solution)/shard_map/pallas_call | solution.py:361
  55.9 0.0 copy-start.3
  55.9 1.2 %slice_bitcast_fusion = f32[96]{0:T(128)} fusion(f32[1,128]{1,0:T(1,128)} %get-tuple-element.15), kind=kLoop, calls=%fused_computation | loop fusion | bytes 768 | tf_op jit(solution)/shard_map/squeeze | solution.py:383
  57.1 0.0 copy-done.2
  57.1 0.0 copy-start.1
  57.1 0.9 %copy.19 = bf16[1,96,8,512]{3,2,1,0:T(8,128)(2,1)} copy(bf16[1,96,8,512]{3,2,1,0:T(8,128)(2,1)S(1)} %bitcast.18) | data formatting | bytes 1572864
  58.0 0.0 copy-done.3
  58.0 0.9 %copy.20 = bf16[1,96,8,512]{3,2,1,0:T(8,128)(2,1)} copy(bf16[1,96,8,512]{3,2,1,0:T(8,128)(2,1)S(1)} %bitcast.19) | data formatting | bytes 1572864
  58.9 0.0 copy-done.1
  58.9 1.1 %copy.21 = f32[27,96,96]{2,1,0:T(8,128)} copy(f32[27,96,96]{2,1,0:T(8,128)S(1)} %copy-done.1) | data formatting | bytes 1990656
Async XLA Ops:
  5.9 1.7 %copy-start = (bf16[27,96,96]{2,1,0:T(8,128)(2,1)S(1)}, bf16[27,96,96]{2,1,0:T(8,128)(2,1)}, u32[]{:S(2)}) copy-start(bf16[27,96,96]{2,1,0:T(8,128)(2,1)} %param.5) | copy-start | bytes 1492996
  25.4 31.7 %copy-start.2 = (bf16[96,8,512]{2,1,0:T(8,128)(2,1)S(1)}, bf16[96,8,512]{2,1,0:T(8,128)(2,1)}, u32[]{:S(2)}) copy-start(bf16[96,8,512]{2,1,0:T(8,128)(2,1)} %get-tuple-element.10) | copy-start | bytes 2359300
  55.9 2.1 %copy-start.3 = (bf16[96,8,512]{2,1,0:T(8,128)(2,1)S(1)}, bf16[96,8,512]{2,1,0:T(8,128)(2,1)}, u32[]{:S(2)}) copy-start(bf16[96,8,512]{2,1,0:T(8,128)(2,1)} %get-tuple-element.13) | copy-start | bytes 2359300
  57.1 1.8 %copy-start.1 = (f32[27,96,96]{2,1,0:T(8,128)S(1)}, f32[27,96,96]{2,1,0:T(8,128)}, u32[]{:S(2)}) copy-start(f32[27,96,96]{2,1,0:T(8,128)} %get-tuple-element.22) | copy-start | bytes 2985988

commit v3 on v2

--- a/solution.py
+++ b/solution.py
@@ -143,8 +143,8 @@
 
 
 def forward_kernel(
-    f_ref, w_ref, b_ref, cot_ref, act_ref, s_ref, sums_ref,
-    tile_ref, x_ref, before_ref, after_ref, patch_ref, acc_ref, cot_rows_ref, wg_ref, sems,
+    f_ref, taps_ref, b_ref, cot_ref, act_ref, s_ref, sums_ref,
+    w_ref, tile_ref, x_ref, before_ref, after_ref, patch_ref, acc_ref, cot_rows_ref, wg_ref, sems,
 ):
     channels, count, cells = f_ref.shape
 
@@ -160,6 +160,11 @@
         "gy", x_ref.at[pl.ds(0, 2)], x_ref.at[pl.ds(count - 2, 2)], before_ref, after_ref, sems
     )
     start()
+    for ty in range(3):
+        for k in range(9):
+            w_ref[
+                ty * channels : (ty + 1) * channels, k * channels : (k + 1) * channels
+            ] = taps_ref[9 * ty + k]
     to_rows(cot_ref, tile_ref, putter(cot_rows_ref))
     seen = set()
     for padded in range(2, count + 2):
@@ -170,7 +175,7 @@
         build(before_ref[row], patch_ref, row)
         build(after_ref[row], patch_ref, count + 2 + row)
     convolve(w_ref, patch_ref, acc_ref, (0, 1, count + 2, count + 3), seen)
-    bias = b_ref[...]
+    bias = jnp.broadcast_to(b_ref[...], (channels, channels)).T[:, :1]
     total = jnp.zeros((channels, 128), jnp.float32)
     for y in range(count):
         for lane in range(cells // 128):
@@ -207,8 +212,8 @@
 
 
 def backward_kernel(
-    s_ref, w_ref, sums_ref, fg_ref, kg_ref, bg_ref,
-    tile_ref, patch_ref, acc_ref, before_ref, after_ref, land1_ref, land2_ref, part_ref, red_ref,
+    s_ref, taps_ref, sums_ref, fg_ref, kg_ref, bg_ref,
+    w_ref, tile_ref, patch_ref, acc_ref, before_ref, after_ref, land1_ref, land2_ref, part_ref, red_ref,
     sems, sends, recvs,
 ):
     channels, count, cells = fg_ref.shape
@@ -250,6 +255,11 @@
         "gy", me_out, outer, 0,
         lambda peer: piece(sums_ref, peer, rows1), lambda k: land1_ref.at[k - 1],
     )
+    for ty in range(3):
+        for k in range(9):
+            w_ref[
+                ty * channels : (ty + 1) * channels, k * channels : (k + 1) * channels
+            ] = taps_ref[26 - 9 * ty - k].astype(jnp.float32).T.astype(jnp.bfloat16)
     for padded in range(2, count + 2):
         build(s_ref[padded - 2], patch_ref, padded)
     seen = set()
@@ -317,15 +327,13 @@
     channels, count, cells = fields.shape[1:]
     x, cot = fields[0], cotangent[0]
     outer, inner = lax.axis_size("gy"), lax.axis_size("dp")
-    taps = kernel_taps.reshape(3, 9, channels, channels)
-    w_fwd = taps.transpose(0, 2, 1, 3).reshape(3 * channels, 9 * channels)
-    w_bwd = taps[::-1, ::-1].transpose(0, 3, 1, 2).reshape(3 * channels, 9 * channels)
     vmem = pl.BlockSpec(memory_space=pltpu.VMEM)
     f32, b16 = jnp.float32, jnp.bfloat16
     tile = pltpu.VMEM((cells // 128, channels * count, 128), f32)
     patch = pltpu.VMEM((count + 4, 9 * channels, cells), b16)
     acc = pltpu.VMEM((count, channels, cells), f32)
     rows = pltpu.VMEM((count, channels, cells), b16)
+    stack = pltpu.VMEM((3 * channels, 9 * channels), b16)
     edge = pltpu.VMEM((2, channels, cells), b16)
     lanes = -(-9 * channels // 128)
     unit = 16 * outer * inner
@@ -349,7 +357,7 @@
         in_specs=[vmem] * 4,
         out_specs=(vmem,) * 3,
         scratch_shapes=[
-            tile, rows, edge, edge, patch, acc, rows,
+            stack, tile, rows, edge, edge, patch, acc, rows,
             pltpu.VMEM((3 * channels, lanes * 128), f32),
             pltpu.SemaphoreType.DMA((4,)),
         ],
@@ -357,7 +365,7 @@
         cost_estimate=pl.CostEstimate(
             flops=2 * flops, bytes_accessed=4000000, transcendentals=0
         ),
-    )(x, w_fwd, bias_vector[:, None], cot)
+    )(x, kernel_taps, bias_vector[None], cot)
     field_grad, kernel_grad, bias_row = pl.pallas_call(
         backward_kernel,
         out_shape=(
@@ -368,7 +376,7 @@
         in_specs=[vmem] * 3,
         out_specs=(vmem,) * 3,
         scratch_shapes=[
-            tile, patch, acc, edge, edge,
+            stack, tile, patch, acc, edge, edge,
             pltpu.VMEM((outer - 1, rows1, 128), b16),
             pltpu.VMEM((inner - 1, rows2, 128), b16),
             pltpu.VMEM((rows1, 128), b16),
@@ -379,7 +387,7 @@
         ],
         compiler_params=params(1),
         cost_estimate=pl.CostEstimate(flops=flops, bytes_accessed=4000000, transcendentals=0),
-    )(slope, w_bwd, sums)
+    )(slope, kernel_taps, sums)
     return activated[None], field_grad[None], kernel_grad, bias_row[0, :channels]
 
 

time: 61 us -> 51.4 us (0.84)
  local copies, waits for them, and re-layouts: 13.9 us -> 4.05 us
    reshape x6 -> x0, local copies, waits for them, and re-layouts: 6.16 us -> none  [the longest x2 2.86 us: shards(): taps = kernel_taps.reshape(3, 9, channels, channels)]
    rev x1 -> x0, local copies, waits for them, and re-layouts: 2.37 us -> none  [shards(): taps[::-1, ::-1].transpose(0, 3, 1, 2).reshape(3 * channels, 9 * channels)]
    broadcast_in_dim x1 -> x0, local copies, waits for them, and re-layouts: 1.37 us -> none  [shards(): bias_vector[:, None]]
    unnamed x11 -> x9, local copies, waits for them, and re-layouts: 2.84 us -> 2.83 us
where the time goes in v3:
time: 51.4 us; the launch traced here: 50.5 us
  Pallas kernels  45.8 us (89%)
  local copies, waits for them, and re-layouts  4.05 us (8%)
  between operations  0.67 us (1%)
    pallas_call x1, Pallas kernels, shards(): pl.pallas_call(backward_kernel, out_shape=(jax.ShapeDtypeStruct((channels...  30.5 us
    pallas_call x1, Pallas kernels, shards(): pl.pallas_call(forward_kernel, out_shape=(jax.ShapeDtypeStruct((channels,...  15.2 us
    unnamed x9, local copies, waits for them, and re-layouts  2.83 us
    squeeze x1, local copies, waits for them, and re-layouts, shards(): bias_row[0, :channels]  1.22 us

profile of v3, /device:TPU:0, one launch (start us, length us, event | category | flops | bytes accessed | tf_op | source)
XLA Modules:
  0.0 50.5 jit_solution(1435695009742966668)
XLA Ops:
  0.6 15.2 %shard_map.75 = (bf16[96,8,512]{2,1,0:T(8,128)(2,1)}, bf16[8,96,512]{2,1,0:T(8,128)(2,1)}, bf16[2048,128]{1,0:T(8,128)(2,1)}) custom-call(bf16[96,8,512]{2,1,0:T(8,128)(2,1)} %bitcast.9, bf16[27,96,96]{2,1,0:T(8,128)(2,1)} %taps_ref.3, f32[1,96]{1,0:T(1,128)} %bitcast.11, bf16[96,8,512]{2,1,0:T(8,128)(2,1)} %bitcast.10), custom_call_target="tpu_custom_call" | custom-call | flops 4076863488 | bytes 4000000 | tf_op jit(solution)/shard_map/pallas_call | solution.py:350
  15.9 0.0 copy-start.1
  15.9 30.5 %shard_map.76 = (bf16[96,8,512]{2,1,0:T(8,128)(2,1)}, f32[27,96,96]{2,1,0:T(8,128)}, f32[1,128]{1,0:T(1,128)}) custom-call(bf16[8,96,512]{2,1,0:T(8,128)(2,1)} %get-tuple-element.11.s_ref, bf16[27,96,96]{2,1,0:T(8,128)(2,1)} %taps_ref.3, bf16[2048,128]{1,0:T(8,128)(2,1)} %get-tuple-element.12.sums_ref), custom_call_target="tpu_custom_call" | custom-call | flops 2038431744 | bytes 4000000 | tf_op jit(solution)/shard_map/pallas_call | solution.py:369
  46.4 0.0 copy-start.2
  46.4 1.2 %slice_bitcast_fusion = f32[96]{0:T(128)} fusion(f32[1,128]{1,0:T(1,128)} %get-tuple-element.15), kind=kLoop, calls=%fused_computation | loop fusion | bytes 768 | tf_op jit(solution)/shard_map/squeeze | solution.py:391
  47.7 0.0 copy-done.1
  47.7 0.0 copy-start
  47.7 0.9 %copy.11 = bf16[1,96,8,512]{3,2,1,0:T(8,128)(2,1)} copy(bf16[1,96,8,512]{3,2,1,0:T(8,128)(2,1)S(1)} %bitcast.7) | data formatting | bytes 1572864
  48.5 0.0 copy-done.2
  48.5 0.9 %copy.12 = bf16[1,96,8,512]{3,2,1,0:T(8,128)(2,1)} copy(bf16[1,96,8,512]{3,2,1,0:T(8,128)(2,1)S(1)} %bitcast.8) | data formatting | bytes 1572864
  49.4 0.0 copy-done
  49.4 1.1 %copy.13 = f32[27,96,96]{2,1,0:T(8,128)} copy(f32[27,96,96]{2,1,0:T(8,128)S(1)} %copy-done) | data formatting | bytes 1990656
Async XLA Ops:
  15.9 31.8 %copy-start.1 = (bf16[96,8,512]{2,1,0:T(8,128)(2,1)S(1)}, bf16[96,8,512]{2,1,0:T(8,128)(2,1)}, u32[]{:S(2)}) copy-start(bf16[96,8,512]{2,1,0:T(8,128)(2,1)} %get-tuple-element.10) | copy-start | bytes 2359300
  46.4 2.1 %copy-start.2 = (bf16[96,8,512]{2,1,0:T(8,128)(2,1)S(1)}, bf16[96,8,512]{2,1,0:T(8,128)(2,1)}, u32[]{:S(2)}) copy-start(bf16[96,8,512]{2,1,0:T(8,128)(2,1)} %get-tuple-element.13) | copy-start | bytes 2359300
  47.7 1.8 %copy-start = (f32[27,96,96]{2,1,0:T(8,128)S(1)}, f32[27,96,96]{2,1,0:T(8,128)}, u32[]{:S(2)}) copy-start(f32[27,96,96]{2,1,0:T(8,128)} %get-tuple-element.22) | copy-start | bytes 2985988
